TPU v7x, 32 devices: a whole 2x2x4 slice. The times are simulated.
32 devices in a mesh: seq: 8 (over y, x, core), ew: 4 (over z).
Axes of the slice: x: 2, y: 2, z: 4, core: 2. Of those that a mesh axis runs over, the one named last changes fastest.
Arguments:
- tokens: bfloat16 [2048, 4096], P('seq', 'ew'), may hold values from -6 to 6
- cotangent: bfloat16 [2048, 4096], P('seq', 'ew'), may hold values from -6 to 6
- w_in: bfloat16 [16384, 4096], P(('seq', 'ew')), may hold values from -0.1875 to 0.1875
- w_out: bfloat16 [16384, 4096], P(('seq', 'ew')), may hold values from -0.1875 to 0.1875
- bar_picks: int32 [4, 256], replicated, may hold values from 0 to 2047, as said below
- gate_weights: float32 [4, 256], replicated, may hold values from 0.2 to 1
Outputs:
- moe_out: bfloat16 [2048, 4096], P('seq', 'ew')
- token_gradient: bfloat16 [2048, 4096], P('seq', 'ew')
Inputs may be any that keep to these rules, and one draw needn't show every extreme that they name: `bar_picks`: each row lists 256 distinct bar tokens. At most 64 of one row's entries lie in one aligned block of 256 bars (the bars of one index of seq), and every row has exactly 64 entries in some block.
All inputs are finite; a program needn't handle non-finite values.
Results may differ from a plain program's by a relative error of at most 0.013.
Values may be sent and summed in bfloat16 or wider, within the bound.
A program may use at most 64 MiB of HBM per device.

v0:
```python
import jax
import jax.numpy as jnp
from jax import lax
from jax.sharding import PartitionSpec as P


def smooth(values):
    return jax.nn.gelu(values, approximate=False)


def per_device(tokens, cotangent, w_in, w_out, bar_picks, gate_weights):
    n_seq = lax.axis_size("seq")
    my_shard = lax.axis_index("seq")
    tok_dev, feat_dev = tokens.shape
    experts = bar_picks.shape[0]
    halves = n_seq // experts
    slot_count = max(2, 2 * tok_dev // n_seq)
    owners = bar_picks // tok_dev
    offsets = bar_picks - owners * tok_dev
    marks = (owners[:, :, None] == jnp.arange(n_seq, dtype=jnp.int32)[None, None, :]).astype(
        jnp.int32
    )
    earlier = jnp.cumsum(marks, axis=1) - marks
    slot_of = jnp.sum(earlier * marks, axis=2)
    is_mine = owners == my_shard
    slot_hit = (
        is_mine[:, :, None]
        & (slot_of[:, :, None] == jnp.arange(slot_count, dtype=jnp.int32)[None, None, :])
    ).astype(jnp.int32)
    filled = jnp.sum(slot_hit, axis=1)
    slot_row = jnp.sum(slot_hit * offsets[:, :, None], axis=1) + (1 - filled) * tok_dev
    slot_dev = jnp.repeat(slot_row, halves, axis=0)
    zero_row = jnp.zeros((1, feat_dev), tokens.dtype)
    send_tok = jnp.concatenate([tokens, zero_row], axis=0)[slot_dev]
    send_grad = jnp.concatenate([cotangent, zero_row], axis=0)[slot_dev]
    recv_tok, received_gradient = (
        lax.all_to_all(send_tok, "seq", split_axis=0, concat_axis=0, tiled=True),
        lax.all_to_all(send_grad, "seq", split_axis=0, concat_axis=0, tiled=True),
    )
    expert = my_shard // halves
    slot_pos = lax.dynamic_index_in_dim(owners * slot_count + slot_of, expert, 0, keepdims=False)
    rows_tok = recv_tok.reshape(n_seq * slot_count, feat_dev)[slot_pos]
    rows_grad = received_gradient.reshape(n_seq * slot_count, feat_dev)[slot_pos]
    full_tok, full_grad = (
        lax.all_gather(rows_tok, "ew", axis=1, tiled=True),
        lax.all_gather(rows_grad, "ew", axis=1, tiled=True),
    )
    contract = (((1,), (1,)), ((), ()))
    hidden = lax.dot_general(full_tok, w_in, contract, preferred_element_type=jnp.float32)
    activated, pull_back = jax.vjp(smooth, hidden)
    slope_in = lax.dot_general(full_grad, w_out, contract, preferred_element_type=jnp.float32)
    back_hidden = pull_back(slope_in)[0].astype(jnp.bfloat16)
    act_bf16 = activated.astype(jnp.bfloat16)
    term_out = jnp.dot(act_bf16, w_out, preferred_element_type=jnp.float32)
    term_grad = jnp.dot(back_hidden, w_in, preferred_element_type=jnp.float32)
    sum_out, sum_grad = (
        lax.psum_scatter(
            term_out.astype(jnp.bfloat16), "ew", scatter_dimension=1, tiled=True
        ).astype(jnp.float32),
        lax.psum_scatter(
            term_grad.astype(jnp.bfloat16), "ew", scatter_dimension=1, tiled=True
        ).astype(jnp.float32),
    )
    gate_col = lax.dynamic_index_in_dim(gate_weights, expert, 0, keepdims=False)[:, None]
    zero_buf = jnp.zeros((n_seq * slot_count, feat_dev), jnp.float32)
    back_out = zero_buf.at[slot_pos].set(gate_col * sum_out).reshape(n_seq, slot_count, feat_dev)
    back_grad = zero_buf.at[slot_pos].set(gate_col * sum_grad).reshape(n_seq, slot_count, feat_dev)
    home_out, home_grad = (
        lax.all_to_all(
            back_out.astype(jnp.bfloat16), "seq", split_axis=0, concat_axis=0, tiled=True
        ).astype(back_out.dtype),
        lax.all_to_all(
            back_grad.astype(jnp.bfloat16), "seq", split_axis=0, concat_axis=0, tiled=True
        ).astype(back_grad.dtype),
    )
    row_ids = slot_dev.reshape(-1)
    combined = jax.ops.segment_sum(
        home_out.reshape(n_seq * slot_count, feat_dev), row_ids, num_segments=tok_dev + 1
    )[:tok_dev]
    combined_grad = jax.ops.segment_sum(
        home_grad.reshape(n_seq * slot_count, feat_dev), row_ids, num_segments=tok_dev + 1
    )[:tok_dev]
    return (combined.astype(jnp.bfloat16), combined_grad.astype(jnp.bfloat16))


def solution(mesh):
    in_specs = (
        P("seq", "ew"),
        P("seq", "ew"),
        P(("seq", "ew"), None),
        P(("seq", "ew"), None),
        P(),
        P(),
    )
    out_specs = (P("seq", "ew"), P("seq", "ew"))
    return jax.shard_map(
        per_device, mesh=mesh, in_specs=in_specs, out_specs=out_specs, check_vma=False
    )
```

profile of v0, /device:TPU:0, one launch (start us, length us, event | category | flops | bytes accessed | tf_op | source)
XLA Modules:
  0.0 262.0 jit_solution(9237293012119956676)
XLA Ops:
  7.2 0.0 copy-start
  7.2 0.7 multiply_subtract_fusion
  7.9 2.3 reduce-window.6
  10.2 0.1 slice.26
  10.3 0.1 copy.12
  10.4 0.1 fusion.28
  10.5 0.2 convert_reduce_fusion
  10.8 0.1 reshape.115
  10.9 1.1 concatenate.6
  11.9 2.8 %gather_fusion = bf16[512,1024]{1,0:T(8,128)(2,1)} fusion(bf16[257,1024]{1,0:T(8,128)(2,1)S(1)} %concatenate.6, s32[1024]{0:T(1024)S(1)} %pad_clamp_fusion.1), kind=kCustom, calls=%fused_computation | custom fusion | bytes 2099200 | tf_op jit(solution)/shard_map/gather | solution.py:34
  14.7 5.2 %all-to-all-start = ((bf16[8,64,1024]{2,1,0:T(8,128)(2,1)}), bf16[8,64,1024]{2,1,0:T(8,128)(2,1)S(1)}, u32[]{:S(2)}, u32[]{:S(2)}) async-start(bf16[8,64,1024]{2,1,0:T(8,128)(2,1)} %bitcast.7), calls=%async_computation | async-start | bytes 2097152 | tf_op jit(solution)/shard_map/all_to_all | solution.py:37
  19.9 0.0 all-gather.5.cloned.1.call-start
  20.0 15.3 %all-to-all-done = bf16[8,64,1024]{2,1,0:T(8,128)(2,1)S(1)} async-done(((bf16[8,64,1024]{2,1,0:T(8,128)(2,1)}), bf16[8,64,1024]{2,1,0:T(8,128)(2,1)S(1)}, u32[]{:S(2)}, u32[]{:S(2)}) %all-to-all-start) | async-done | bytes 1048608 | tf_op jit(solution)/shard_map/all_to_all | solution.py:37
  35.3 0.0 copy-start.1
  35.3 2.0 gather_fusion.1
  37.3 0.0 all-gather.5.cloned.1.call-update
  37.3 0.0 all-gather.7.cloned.1.call-start
  37.3 0.0 copy-done.1
  37.4 2.1 gather_fusion.2
  39.5 17.8 %all_to_all.20 = bf16[8,64,1024]{2,1,0:T(8,128)(2,1)S(1)} all-to-all(bf16[8,64,1024]{2,1,0:T(8,128)(2,1)S(1)} %bitcast.40), channel_id=1, replica_groups=mesh['seq'=8,'ew'=4] {'seq'}, dimensions={0} | all-to-all | bytes 2097152 | tf_op jit(solution)/shard_map/all_to_all | solution.py:38
  57.3 2.0 gather_fusion.3
  59.2 0.0 all-gather.7.cloned.1.call-update
  59.2 0.0 reduce-scatter.5.cloned.1.call-start
  59.3 23.5 %all-gather.5.cloned.1.call-done = bf16[256,4096]{1,0:T(8,128)(2,1)} async-done(((bf16[256,1024]{1,0:T(8,128)(2,1)}), bf16[256,4096]{1,0:T(8,128)(2,1)}) %all-gather.5.cloned.1.call-update) | async-done | bytes 2097168 | tf_op jit(solution)/shard_map/all_gather | solution.py:45
  82.8 4.1 %fusion.43 = f32[256,512]{1,0:T(8,128)S(1)} fusion(bf16[256,4096]{1,0:T(8,128)(2,1)} %all-gather.5.cloned.1.call-done, bf16[512,4096]{1,0:T(8,128)(2,1)} %param.8), kind=kOutput, calls=%fused_computation.84 | convolution fusion | flops 1073741824 | bytes 6815744 | tf_op jit(solution)/shard_map/dot_general | solution.py:49
  86.9 42.6 %all-gather.7.cloned.1.call-done = bf16[256,4096]{1,0:T(8,128)(2,1)} async-done(((bf16[256,1024]{1,0:T(8,128)(2,1)}), bf16[256,4096]{1,0:T(8,128)(2,1)}) %all-gather.7.cloned.1.call-update) | async-done | bytes 2097168 | tf_op jit(solution)/shard_map/all_gather | solution.py:46
  129.6 8.9 %convolution_convert_fusion = bf16[256,4096]{1,0:T(8,128)(2,1)} fusion(bf16[512,4096]{1,0:T(8,128)(2,1)} %param.8, f32[256,512]{1,0:T(8,128)S(1)} %fusion.43, bf16[256,4096]{1,0:T(8,128)(2,1)} %all-gather.7.cloned.1.call-done, bf16[512,4096]{1,0:T(8,128)(2,1)} %param.9), kind=kOutput, calls=%fused_computation.8 | convolution fusion | flops 2157969408 | bytes 13107200 | tf_op jit(solution)/shard_map/dot_general | solution.py:55
  138.5 0.0 reduce-scatter.5.cloned.1.call-update
  138.5 0.2 reduce-scatter.3.cloned.1.call-start
  138.7 5.8 %convolution_convert_fusion.1 = bf16[256,4096]{1,0:T(8,128)(2,1)} fusion(bf16[512,4096]{1,0:T(8,128)(2,1)} %param.9, f32[256,512]{1,0:T(8,128)S(1)} %fusion.43), kind=kOutput, calls=%fused_computation.9 | convolution fusion | flops 1083310080 | bytes 6815744 | tf_op jit(solution)/shard_map/dot_general | solution.py:54
  144.5 0.0 reduce-scatter.3.cloned.1.call-update
  144.6 0.0 copy-done
  144.6 36.6 %reduce-scatter.5.cloned.1.call-done = bf16[256,1024]{1,0:T(8,128)(2,1)} async-done(((bf16[256,4096]{1,0:T(8,128)(2,1)}), bf16[256,1024]{1,0:T(8,128)(2,1)}) %reduce-scatter.5.cloned.1.call-update) | async-done | bytes 524304 | tf_op jit(solution)/shard_map/reduce_scatter | solution.py:60
  181.2 2.6 scatter_custom_fusion.2
  183.8 1.1 convert_element_type.55
  184.9 3.7 %all-to-all-start.3 = ((bf16[8,64,1024]{2,1,0:T(8,128)(2,1)}), bf16[8,64,1024]{2,1,0:T(8,128)(2,1)S(1)}, u32[]{:S(2)}, u32[]{:S(2)}) async-start(bf16[8,64,1024]{2,1,0:T(8,128)(2,1)} %bitcast.13), calls=%async_computation.5 | async-start | bytes 2097152 | tf_op jit(solution)/shard_map/all_to_all | solution.py:72
  188.6 38.1 %reduce-scatter.3.cloned.1.call-done = bf16[256,1024]{1,0:T(8,128)(2,1)} async-done(((bf16[256,4096]{1,0:T(8,128)(2,1)}), bf16[256,1024]{1,0:T(8,128)(2,1)}) %reduce-scatter.3.cloned.1.call-update) | async-done | bytes 524304 | tf_op jit(solution)/shard_map/reduce_scatter | solution.py:57
  226.7 2.6 scatter_custom_fusion
  229.3 1.1 convert_element_type.50
  230.4 0.0 all-to-all-done.3
  230.4 3.7 %all-to-all-start.1 = ((bf16[8,64,1024]{2,1,0:T(8,128)(2,1)}), bf16[8,64,1024]{2,1,0:T(8,128)(2,1)S(1)}, u32[]{:S(2)}, u32[]{:S(2)}) async-start(bf16[8,64,1024]{2,1,0:T(8,128)(2,1)} %bitcast.9), calls=%async_computation.2 | async-start | bytes 2097152 | tf_op jit(solution)/shard_map/all_to_all | solution.py:69
  234.1 0.1 reshape.155
  234.2 5.3 %scatter_custom_fusion.3 = f32[257,1024]{1,0:T(8,128)S(1)} fusion(s32[512]{0:T(512)S(1)} %reshape.155, bf16[512,1024]{1,0:T(8,128)(2,1)S(1)} %bitcast.41, f32[]{:T(128)} %constant.44.clone.1), kind=kCustom, calls=%fused_computation.10 | custom fusion | flops 1048576 | bytes 2101252 | tf_op jit(solution)/shard_map/scatter-add | solution.py:80
  239.5 0.9 slice.32
  240.3 9.2 %all-to-all-done.1 = bf16[8,64,1024]{2,1,0:T(8,128)(2,1)S(1)} async-done(((bf16[8,64,1024]{2,1,0:T(8,128)(2,1)}), bf16[8,64,1024]{2,1,0:T(8,128)(2,1)S(1)}, u32[]{:S(2)}, u32[]{:S(2)}) %all-to-all-start.1) | async-done | bytes 1048608 | tf_op jit(solution)/shard_map/all_to_all | solution.py:69
  249.5 5.1 %scatter_custom_fusion.1 = f32[257,1024]{1,0:T(8,128)S(1)} fusion(s32[512]{0:T(512)S(1)} %reshape.155, bf16[512,1024]{1,0:T(8,128)(2,1)S(1)} %bitcast.42, f32[]{:T(128)} %constant.44.clone.1), kind=kCustom, calls=%fused_computation.12 | custom fusion | flops 1048576 | bytes 2101252 | tf_op jit(solution)/shard_map/scatter-add | solution.py:77
  254.6 0.9 slice.33
  (14 shorter events, 0.1 us)
Async XLA Ops:
  7.2 137.4 %copy-start = (f32[4,256]{1,0:T(4,128)S(1)}, f32[4,256]{1,0:T(4,128)}, u32[]{:S(2)}) copy-start(f32[4,256]{1,0:T(4,128)} %param.11) | copy-start | bytes 12292
  14.7 20.6 %all-to-all-start = ((bf16[8,64,1024]{2,1,0:T(8,128)(2,1)}), bf16[8,64,1024]{2,1,0:T(8,128)(2,1)S(1)}, u32[]{:S(2)}, u32[]{:S(2)}) async-start(bf16[8,64,1024]{2,1,0:T(8,128)(2,1)} %bitcast.7), calls=%async_computation | async-start | bytes 2097152 | tf_op jit(solution)/shard_map/all_to_all | solution.py:37
  19.9 62.9 %all-gather.5.cloned.1.call-start = ((), (), s32[]{:S(2)}) async-start(), calls=%async_computation.8 | async-start | bytes 2621440 | tf_op jit(solution)/shard_map/all_gather | solution.py:45
  35.3 2.0 copy-start.1
  37.3 92.3 %all-gather.7.cloned.1.call-start = ((), (), s32[]{:S(2)}) async-start(), calls=%async_computation.9 | async-start | bytes 2621440 | tf_op jit(solution)/shard_map/all_gather | solution.py:46
  59.2 122.0 %reduce-scatter.5.cloned.1.call-start = ((), (), s32[]{:S(2)}) async-start(), calls=%async_computation.7 | async-start | bytes 2621440 | tf_op jit(solution)/shard_map/reduce_scatter | solution.py:60
  138.5 88.2 %reduce-scatter.3.cloned.1.call-start = ((), (), s32[]{:S(2)}) async-start(), calls=%async_computation.6 | async-start | bytes 2621440 | tf_op jit(solution)/shard_map/reduce_scatter | solution.py:57
  184.9 45.5 %all-to-all-start.3 = ((bf16[8,64,1024]{2,1,0:T(8,128)(2,1)}), bf16[8,64,1024]{2,1,0:T(8,128)(2,1)S(1)}, u32[]{:S(2)}, u32[]{:S(2)}) async-start(bf16[8,64,1024]{2,1,0:T(8,128)(2,1)} %bitcast.13), calls=%async_computation.5 | async-start | bytes 2097152 | tf_op jit(solution)/shard_map/all_to_all | solution.py:72
  230.4 19.1 %all-to-all-start.1 = ((bf16[8,64,1024]{2,1,0:T(8,128)(2,1)}), bf16[8,64,1024]{2,1,0:T(8,128)(2,1)S(1)}, u32[]{:S(2)}, u32[]{:S(2)}) async-start(bf16[8,64,1024]{2,1,0:T(8,128)(2,1)} %bitcast.9), calls=%async_computation.2 | async-start | bytes 2097152 | tf_op jit(solution)/shard_map/all_to_all | solution.py:69
Sparse Core Ops, SparseCore 0:
  37.4 45.3 all-gather.4
  84.9 44.5 all-gather.6
  138.6 42.5 reduce-scatter.4
  183.5 43.1 reduce-scatter.2
where the time goes:
time: 263 us; the launch traced here: 262 us
  waiting for transfers between devices  165 us (63%)
  other arithmetic  21.1 us (8%)
  matrix products  18.8 us (7%)
  blocking collectives  17.8 us (7%)
  between operations  13.9 us (5%)
  starting transfers between devices  12.8 us (5%)
  local copies, waits for them, and re-layouts  12 us (5%)
    all_gather x1, waiting for transfers between devices, per_device(): lax.all_gather(rows_grad, 'ew', axis=1, tiled=True)  42.6 us
    reduce_scatter x1, waiting for transfers between devices, per_device(): lax.psum_scatter(term_out.astype(jnp.bfloat16), 'ew', scatter_dimension=1...  38.1 us
    reduce_scatter x1, waiting for transfers between devices, per_device(): lax.psum_scatter(term_grad.astype(jnp.bfloat16), 'ew', scatter_dimension=...  36.6 us
    all_gather x1, waiting for transfers between devices, per_device(): lax.all_gather(rows_tok, 'ew', axis=1, tiled=True)  23.5 us
    all_to_all x1, blocking collectives, per_device(): lax.all_to_all(send_grad, 'seq', split_axis=0, concat_axis=0, tiled=True)  17.8 us
    all_to_all x1, waiting for transfers between devices, per_device(): lax.all_to_all(send_tok, 'seq', split_axis=0, concat_axis=0, tiled=True)  15.3 us
    all_to_all x1, waiting for transfers between devices, per_device(): lax.all_to_all(back_out.astype(jnp.bfloat16), 'seq', split_axis=0, concat...  9.17 us
    dot_general x1, matrix products, per_device(): term_grad = jnp.dot(back_hidden, w_in, preferred_element_type=jnp.float32)  8.92 us
  transfers between devices with their start and end apart: 7, of which 6 were waited for; matrix products, arithmetic and copies ran while one was open for 11% of the time, Pallas kernels for 0%

commit v1 on v0

v1 whole, which is shorter than its diff:
```python
import functools
import math

import jax
import jax.numpy as jnp
from jax import lax
from jax.experimental import pallas as pl
from jax.experimental.pallas import tpu as pltpu
from jax.sharding import PartitionSpec as P

MESH = pl.DeviceIdType.MESH
F32 = jnp.float32
BF16 = jnp.bfloat16


def iota(shape, dim):
    return lax.broadcasted_iota(jnp.int32, shape, dim).astype(F32)


def to_column(row):
    n = row.shape[1]
    return jnp.sum(jnp.where(iota((n, n), 0) == iota((n, n), 1), row, 0.0), axis=1, keepdims=True)


def to_row(col):
    n = col.shape[0]
    return jnp.sum(jnp.where(iota((n, n), 0) == iota((n, n), 1), col, 0.0), axis=0, keepdims=True)


def dot(a, b, dims=(1, 0)):
    return lax.dot_general(
        a, b, (((dims[0],), (dims[1],)), ((), ())), preferred_element_type=F32
    )


def kernel(
    rows, n_seq, n_ew,
    tok_ref, cot_ref, win_ref, wout_ref, picks_ref, gates_ref,
    out_ref, grad_ref,
    wv, pk, uu, gcol, send, recv, full, hid, slo, hb, px, own, xch,
    ard, aru, sdn, sup, total, bsend, home,
    wsem, as_, ar_, ps_, pr_, gds, gdr, gus, gur, xs_, xr_, rds, rdr, rus, rur, bs_, br_,
):
    me = lax.axis_index("seq")
    z = lax.axis_index("ew")
    k = lax.rem(me, 2)
    e_me = lax.div(me, 2)
    partner = me + 1 - 2 * k
    experts, cap = picks_ref.shape
    tok, feat = tok_ref.shape
    slots = send.shape[3]
    starts = [sum(rows[:r]) for r in range(2)]
    last = n_ew - 1
    span = [pl.ds(starts[r], rows[r]) for r in range(2)]

    barrier = pltpu.get_barrier_semaphore()
    for i in range(1, n_seq):
        pl.semaphore_signal(
            barrier, inc=1, device_id=(lax.rem(me + i, n_seq), z), device_id_type=MESH
        )

    @pl.when(z > 0)
    def _():
        pl.semaphore_signal(barrier, inc=1, device_id=(me, z - 1), device_id_type=MESH)

    @pl.when(z < last)
    def _():
        pl.semaphore_signal(barrier, inc=1, device_id=(me, z + 1), device_id_type=MESH)

    w_copies = [
        pltpu.make_async_copy(wout_ref, wv.at[0], wsem.at[0]),
        pltpu.make_async_copy(win_ref, wv.at[1], wsem.at[1]),
    ]
    for c in w_copies:
        c.start()

    base = (me * tok).astype(F32)
    t_col = iota((tok, cap), 0) + base
    for e in range(experts):
        pick = picks_ref[e : e + 1, :].astype(F32)
        hit = jnp.sum(jnp.where(pick == t_col, 1.0, 0.0), axis=1, keepdims=True)
        rank = jnp.sum(
            jnp.where((pick >= base) & (pick < t_col), 1.0, 0.0), axis=1, keepdims=True
        )
        key = to_row(jnp.where(hit > 0.0, rank, -1.0))
        for r in range(2):
            want = 2.0 * iota((slots, tok), 0) + float(r)
            pk[r, e] = jnp.where(want == key, 1.0, 0.0).astype(BF16)

    inside = (z > 0) & (z < last)

    @pl.when(inside)
    def _():
        pl.semaphore_wait(barrier, n_seq + 1)

    @pl.when(jnp.logical_not(inside))
    def _():
        pl.semaphore_wait(barrier, n_seq)

    def remote(src, dst, s, r, dev):
        return pltpu.make_async_remote_copy(
            src_ref=src, dst_ref=dst, send_sem=s, recv_sem=r, device_id=dev, device_id_type=MESH
        )

    def dispatch(r, i):
        d = lax.rem(me + i, n_seq)
        return remote(
            send.at[r, lax.rem(d, 2), lax.div(d, 2)], recv.at[r, me],
            as_.at[r, i], ar_.at[r, i], (d, z),
        )

    for r in range(2):
        sel = pk[r].reshape(experts * slots, tok)
        send[r, 0] = dot(sel, tok_ref[...]).astype(BF16).reshape(experts, slots, feat)
        send[r, 1] = dot(sel, cot_ref[...]).astype(BF16).reshape(experts, slots, feat)
        for i in range(1, n_seq):
            dispatch(r, i).start()
        recv[r, me] = send[r, k, e_me]

    pick = picks_ref[pl.ds(e_me, 1), :].astype(F32)
    gate = to_column(gates_ref[pl.ds(e_me, 1), :])
    pick_c = to_column(pick)
    owner = jnp.floor((pick + 0.5) * (1.0 / tok))
    owner_c = jnp.floor((pick_c + 0.5) * (1.0 / tok))
    rank_c = jnp.sum(
        jnp.where((owner == owner_c) & (pick < pick_c), 1.0, 0.0), axis=1, keepdims=True
    )
    half_c = jnp.floor(rank_c * 0.5)
    slot_c = owner_c * float(slots) + half_c
    parity = rank_c - 2.0 * half_c
    wide = n_seq * slots
    before = jnp.where(iota((wide, wide), 0) < iota((wide, wide), 1), 1.0, 0.0).astype(BF16)
    for r in range(2):
        here = jnp.where(parity == float(r), slot_c, -1.0)
        match = here == iota((cap, wide), 1)
        valid = jnp.sum(jnp.where(match, 1.0, 0.0), axis=0, keepdims=True)
        gate_pad = jnp.sum(jnp.where(match, gate, 0.0), axis=0, keepdims=True)
        place = dot(jnp.broadcast_to(valid, (16, wide)).astype(BF16), before)[0:1]
        place = jnp.where(valid > 0.0, place, -1.0)
        pick_out = iota((rows[r], wide), 0) == place
        uu[span[r], :] = jnp.where(pick_out, 1.0, 0.0).astype(BF16)
        gcol[span[r], :] = jnp.sum(jnp.where(pick_out, gate_pad, 0.0), axis=1, keepdims=True)

    def compact(r):
        for i in range(1, n_seq):
            dispatch(r, i).wait_recv()
        full[k, z, span[r], :] = dot(
            uu[span[r], :], recv[r].reshape(wide, feat)
        ).astype(BF16)

    def g_down(r, h):
        ref = full.at[k, z + h, span[r]]
        return remote(ref, ref, gds.at[r, h], gdr.at[r, h], (me, z - 1))

    def g_up(r, h):
        ref = full.at[k, z - h, span[r]]
        return remote(ref, ref, gus.at[r, h], gur.at[r, h], (me, z + 1))

    def g_down_in(r, h):
        ref = full.at[k, z + 1 + h, span[r]]
        return remote(ref, ref, gds.at[r, h], gdr.at[r, h], (me, z + 1))

    def g_up_in(r, h):
        ref = full.at[k, z - 1 - h, span[r]]
        return remote(ref, ref, gus.at[r, h], gur.at[r, h], (me, z - 1))

    def g_pair(r, s, i, arr):
        ref = full.at[arr, s, span[r]]
        return remote(ref, ref, ps_.at[r, i], pr_.at[r, i], (partner, z))

    def gather_start(r):
        @pl.when(z > 0)
        def _():
            g_down(r, 0).start()

        @pl.when(z < last)
        def _():
            g_up(r, 0).start()

        g_pair(r, z, 0, k).start()

    def gather_arrive(r, h):
        @pl.when(z + 1 + h <= last)
        def _():
            g_down_in(r, h).wait_recv()
            if h + 1 <= last - 1:
                @pl.when(z > 0)
                def _():
                    g_down(r, h + 1).start()

            g_pair(r, z + 1 + h, 1 + 2 * h, k).start()

        @pl.when(z - 1 - h >= 0)
        def _():
            g_up_in(r, h).wait_recv()
            if h + 1 <= last - 1:
                @pl.when(z < last)
                def _():
                    g_up(r, h + 1).start()

            g_pair(r, z - 1 - h, 2 + 2 * h, k).start()

    def pair_each(r, arr, what):
        what(g_pair(r, z, 0, arr))
        for h in range(last):
            @pl.when(z + 1 + h <= last)
            def _():
                what(g_pair(r, z + 1 + h, 1 + 2 * h, arr))

            @pl.when(z - 1 - h >= 0)
            def _():
                what(g_pair(r, z - 1 - h, 2 + 2 * h, arr))

    def x_pair(r, j):
        return remote(
            px.at[j, span[r]], xch.at[j, span[r]], xs_.at[r, j], xr_.at[r, j], (partner, z)
        )

    def compute(r):
        n = rows[r]
        pair_each(r, 1 - k, lambda c: c.wait_recv())
        hid[0:n, :] = jnp.zeros((n, hid.shape[1]), F32)
        slo[0:n, :] = jnp.zeros((n, slo.shape[1]), F32)

        def into(s, carry):
            cols = pl.ds(pl.multiple_of(s * feat, feat), feat)
            hid[0:n, :] += dot(full[0, s, span[r], :], wv[1, :, cols], (1, 1))
            slo[0:n, :] += dot(full[1, s, span[r], :], wv[0, :, cols], (1, 1))
            return carry

        lax.fori_loop(0, n_ew, into, 0)
        x = hid[0:n, :]
        cdf = 0.5 * (1.0 + lax.erf(x * math.sqrt(0.5)))
        pdf = jnp.exp(-0.5 * x * x) * (1.0 / math.sqrt(2.0 * math.pi))
        hb[0, 0:n, :] = (x * cdf).astype(BF16)
        hb[1, 0:n, :] = (slo[0:n, :] * (cdf + x * pdf)).astype(BF16)

        def other(j, carry):
            cols = pl.ds(pl.multiple_of(j * feat, feat), feat)
            px[j, span[r], :] = dot(hb[1 - k, 0:n, :], wv[1 - k, :, cols]).astype(BF16)
            x_pair(r, j).start()
            return carry

        lax.fori_loop(0, n_ew, other, 0)

        def mine(j, carry):
            cols = pl.ds(pl.multiple_of(j * feat, feat), feat)
            own[j, span[r], :] = dot(hb[k, 0:n, :], wv[k, :, cols]).astype(BF16)
            return carry

        lax.fori_loop(0, n_ew, mine, 0)

    def r_down(r, j, t):
        return remote(sdn.at[j, span[r]], ard.at[j, span[r]], rds.at[r, t], rdr.at[r, t], (me, z - 1))

    def r_up(r, j, t):
        return remote(sup.at[j, span[r]], aru.at[j, span[r]], rus.at[r, t], rur.at[r, t], (me, z + 1))

    def r_down_in(r, j, t):
        return remote(sdn.at[j, span[r]], ard.at[j, span[r]], rds.at[r, t], rdr.at[r, t], (me, z + 1))

    def r_up_in(r, j, t):
        return remote(sup.at[j, span[r]], aru.at[j, span[r]], rus.at[r, t], rur.at[r, t], (me, z - 1))

    def pair_sum(r, j):
        x_pair(r, j).wait_recv()
        return own[j, span[r], :].astype(F32) + xch[j, span[r], :].astype(F32)

    def reduce_step(r, t):
        jd = t - (last - z)

        @pl.when((jd >= 0) & (jd < z))
        def _():
            @pl.when(z == last)
            def _():
                sdn[jd, span[r], :] = pair_sum(r, jd).astype(BF16)

            if t >= 1:
                @pl.when(z < last)
                def _():
                    r_down_in(r, jd, t - 1).wait_recv()
                    sdn[jd, span[r], :] = (
                        pair_sum(r, jd) + ard[jd, span[r], :].astype(F32)
                    ).astype(BF16)

            r_down(r, jd, t).start()

        ju = last - (t - z)

        @pl.when((ju > z) & (ju <= last))
        def _():
            @pl.when(z == 0)
            def _():
                sup[ju, span[r], :] = pair_sum(r, ju).astype(BF16)

            if t >= 1:
                @pl.when(z > 0)
                def _():
                    r_up_in(r, ju, t - 1).wait_recv()
                    sup[ju, span[r], :] = (
                        pair_sum(r, ju) + aru[ju, span[r], :].astype(F32)
                    ).astype(BF16)

            r_up(r, ju, t).start()

    def give_back(r, i):
        d = lax.rem(me + i, n_seq)
        return remote(
            bsend.at[r, d], home.at[k, r, e_me], bs_.at[r, i], br_.at[r, i], (d, z)
        )

    def give_back_in(r, i):
        s = lax.rem(me + n_seq - i, n_seq)
        return remote(
            bsend.at[r, me], home.at[lax.rem(s, 2), r, lax.div(s, 2)],
            bs_.at[r, i], br_.at[r, i], (s, z),
        )

    def finish(r):
        n = rows[r]
        total[0:n, :] = pair_sum(r, z)

        @pl.when(z < last)
        def _():
            r_down_in(r, z, last - 1).wait_recv()
            total[0:n, :] += ard[z, span[r], :].astype(F32)

        @pl.when(z > 0)
        def _():
            r_up_in(r, z, last - 1).wait_recv()
            total[0:n, :] += aru[z, span[r], :].astype(F32)

        term = (gcol[span[r], :] * total[0:n, :]).astype(BF16)
        bsend[r] = dot(uu[span[r], :], term, (0, 0)).astype(BF16).reshape(n_seq, slots, feat)
        for i in range(1, n_seq):
            give_back(r, i).start()
        home[k, r, e_me] = bsend[r, me]

    compact(0)
    gather_start(0)
    compact(1)
    for h in range(last - 1):
        gather_arrive(0, h)
    gather_start(1)
    gather_arrive(0, last - 1)
    for c in w_copies:
        c.wait()
    compute(0)
    for t in range(last):
        gather_arrive(1, t)
        reduce_step(0, t)
    compute(1)
    finish(0)
    for t in range(last):
        reduce_step(1, t)
    finish(1)

    for r in range(2):
        for i in range(1, n_seq):
            give_back_in(r, i).wait_recv()
    sel = pk[...].reshape(2 * experts * slots, tok)
    out_ref[...] = dot(sel, home[0].reshape(2 * experts * slots, feat), (0, 0)).astype(BF16)
    grad_ref[...] = dot(sel, home[1].reshape(2 * experts * slots, feat), (0, 0)).astype(BF16)

    for r in range(2):
        for i in range(1, n_seq):
            dispatch(r, i).wait_send()
            give_back(r, i).wait_send()
        pair_each(r, k, lambda c: c.wait_send())
        for j in range(n_ew):
            x_pair(r, j).wait_send()
        for h in range(last):
            @pl.when((z > 0) & (z + h <= last))
            def _():
                g_down(r, h).wait_send()

            @pl.when((z < last) & (z - h >= 0))
            def _():
                g_up(r, h).wait_send()

            jd = h - (last - z)

            @pl.when((jd >= 0) & (jd < z))
            def _():
                r_down(r, jd, h).wait_send()

            ju = last - (h - z)

            @pl.when((ju > z) & (ju <= last))
            def _():
                r_up(r, ju, h).wait_send()


def per_device(tokens, cotangent, w_in, w_out, bar_picks, gate_weights):
    n_seq = lax.axis_size("seq")
    n_ew = lax.axis_size("ew")
    tok, feat = tokens.shape
    ff, depth = w_in.shape
    experts, cap = bar_picks.shape
    most = max(2, 2 * tok // n_seq)
    slots = -(-((most + 1) // 2) // 16) * 16
    rows = (-(-((cap + n_seq) // 2) // 16) * 16, -(-(cap // 2) // 16) * 16)
    both, top = sum(rows), max(rows)
    dma = pltpu.SemaphoreType.DMA
    vmem = pl.BlockSpec(memory_space=pltpu.VMEM)
    hbm = pl.BlockSpec(memory_space=pl.ANY)
    shape = jax.ShapeDtypeStruct((tok, feat), BF16)
    shards = pltpu.VMEM((n_ew, both, feat), BF16)
    steps = max(1, n_ew - 1)
    return tuple(
        pl.pallas_call(
            functools.partial(kernel, rows, n_seq, n_ew),
            out_shape=(shape, shape),
            in_specs=[vmem, vmem, hbm, hbm, vmem, vmem],
            out_specs=(vmem, vmem),
            scratch_shapes=[
                pltpu.VMEM((2, ff, depth), BF16),
                pltpu.VMEM((2, experts, slots, tok), BF16),
                pltpu.VMEM((both, n_seq * slots), BF16),
                pltpu.VMEM((both, 1), F32),
                pltpu.VMEM((2, 2, experts, slots, feat), BF16),
                pltpu.VMEM((2, n_seq, slots, feat), BF16),
                pltpu.VMEM((2, n_ew, both, feat), BF16),
                pltpu.VMEM((top, ff), F32),
                pltpu.VMEM((top, ff), F32),
                pltpu.VMEM((2, top, ff), BF16),
                shards, shards, shards,
                shards, shards, shards, shards,
                pltpu.VMEM((top, feat), F32),
                pltpu.VMEM((2, n_seq, slots, feat), BF16),
                pltpu.VMEM((2, 2, experts, slots, feat), BF16),
                dma((2,)),
                dma((2, n_seq)), dma((2, n_seq)),
                dma((2, 2 * steps + 1)), dma((2, 2 * steps + 1)),
                dma((2, steps)), dma((2, steps)), dma((2, steps)), dma((2, steps)),
                dma((2, n_ew)), dma((2, n_ew)),
                dma((2, steps)), dma((2, steps)), dma((2, steps)), dma((2, steps)),
                dma((2, n_seq)), dma((2, n_seq)),
            ],
            compiler_params=pltpu.CompilerParams(
                collective_id=0, has_side_effects=True, vmem_limit_bytes=56 * 1024 * 1024
            ),
        )(tokens, cotangent, w_in, w_out, bar_picks, gate_weights)
    )


def solution(mesh):
    in_specs = (
        P("seq", "ew"),
        P("seq", "ew"),
        P(("seq", "ew"), None),
        P(("seq", "ew"), None),
        P(),
        P(),
    )
    out_specs = (P("seq", "ew"), P("seq", "ew"))
    return jax.shard_map(
        per_device, mesh=mesh, in_specs=in_specs, out_specs=out_specs, check_vma=False
    )
```

time: 263 us -> 104 us (0.40)
  waiting for transfers between devices: 165 us -> 0 us
  Pallas kernels: 0 us -> 99.5 us
  other arithmetic: 21.1 us -> 0 us
  matrix products: 18.8 us -> 0 us
  blocking collectives: 17.8 us -> 0 us
  between operations: 13.9 us -> 0.64 us
  starting transfers between devices: 12.8 us -> 0 us
  local copies, waits for them, and re-layouts: 12 us -> 3.74 us
    pallas_call x0 -> x1, Pallas kernels: none -> 99.5 us  [per_device(): pl.pallas_call(functools.partial(kernel, rows, n_seq, n_ew), out_shape=(s...]
    reduce_scatter x2 -> x0, waiting for transfers between devices: 74.7 us -> none  [the longest x1 38.1 us: per_device(): lax.psum_scatter(term_out.astype(jnp.bfloat16), 'ew', scatter_dimension=1...]
    all_gather x2 -> x0, waiting for transfers between devices: 66.1 us -> none  [the longest x1 42.6 us: per_device(): lax.all_gather(rows_grad, 'ew', axis=1, tiled=True)]
    all_to_all x3 -> x0, waiting for transfers between devices: 24.5 us -> none  [the longest x1 15.3 us: per_device(): lax.all_to_all(send_tok, 'seq', split_axis=0, concat_axis=0, tiled=True)]
    dot_general x3 -> x0, matrix products: 18.8 us -> none  [the longest x1 8.92 us: per_device(): term_grad = jnp.dot(back_hidden, w_in, preferred_element_type=jnp.float32)]
    all_to_all x1 -> x0, blocking collectives: 17.8 us -> none  [per_device(): lax.all_to_all(send_grad, 'seq', split_axis=0, concat_axis=0, tiled=True)]
    all_to_all x3 -> x0, starting transfers between devices: 12.5 us -> none  [the longest x1 5.17 us: per_device(): lax.all_to_all(send_tok, 'seq', split_axis=0, concat_axis=0, tiled=True)]
    scatter-add x2 -> x0, other arithmetic: 10.3 us -> none  [the longest x1 5.28 us: per_device(): jax.ops.segment_sum(home_grad.reshape(n_seq * slot_count, feat_dev), row_...]
  transfers between devices with their start and end apart: 7 -> 0, of which waited for: 6 -> 0; matrix products, arithmetic and copies ran while one was open for 11% -> 0% of each run, Pallas kernels for 0% -> 0%
where the time goes in v1:
time: 104 us
  Pallas kernels  99.5 us (96%)
  local copies, waits for them, and re-layouts  3.74 us (4%)
    pallas_call x1, Pallas kernels, per_device(): pl.pallas_call(functools.partial(kernel, rows, n_seq, n_ew), out_shape=(s...  99.5 us
    unnamed x2, local copies, waits for them, and re-layouts  3.74 us

profile of v1, /device:TPU:0, one launch (start us, length us, event | category | flops | bytes accessed | tf_op | source)
XLA Modules:
  0.0 103.9 jit_solution(4375260055196314068)
XLA Ops:
  0.6 99.5 %shard_map.77 = (bf16[256,1024]{1,0:T(8,128)(2,1)}, bf16[256,1024]{1,0:T(8,128)(2,1)}) custom-call(bf16[256,1024]{1,0:T(8,128)(2,1)} %tok_ref.1, bf16[256,1024]{1,0:T(8,128)(2,1)} %cot_ref.1, bf16[512,4096]{1,0:T(8,128)(2,1)} %win_ref.1, bf16[512,4096]{1,0:T(8,128)(2,1)} %wout_ref.1, s32[4,256]{1,0:T(4,128)} %picks_ref.1, f32[4,256]{1,0:T(4,128)} %gates_ref.1), custom_call_target="tpu_custom_call" | custom-call | tf_op jit(solution)/shard_map/pallas_call | solution.py:411
  100.2 1.9 %copy.10 = bf16[256,1024]{1,0:T(8,128)(2,1)} copy(bf16[256,1024]{1,0:T(8,128)(2,1)} %get-tuple-element.4) | data formatting | bytes 1048576
  102.0 1.9 %copy.11 = bf16[256,1024]{1,0:T(8,128)(2,1)} copy(bf16[256,1024]{1,0:T(8,128)(2,1)} %get-tuple-element.5) | data formatting | bytes 1048576

commit v2 on v1

v2 whole, which is shorter than its diff:
```python
import functools
import math

import jax
import jax.numpy as jnp
from jax import lax
from jax.experimental import pallas as pl
from jax.experimental.pallas import tpu as pltpu
from jax.sharding import PartitionSpec as P

MESH = pl.DeviceIdType.MESH
F32 = jnp.float32
BF16 = jnp.bfloat16


def iota(shape, dim):
    return lax.broadcasted_iota(jnp.int32, shape, dim).astype(F32)


def columns(*rows):
    fill = jnp.zeros((8 - len(rows), rows[0].shape[1]), F32)
    return jnp.transpose(jnp.concatenate(rows + (fill,), axis=0))


def dot(a, b, dims=(1, 0)):
    return lax.dot_general(
        a, b, (((dims[0],), (dims[1],)), ((), ())), preferred_element_type=F32
    )


def kernel(
    rows, n_seq, n_ew,
    tok_ref, cot_ref, win_ref, wout_ref, picks_ref, gates_ref,
    out_ref, grad_ref,
    wv, pk, uu, gcol, send, recv, full, hid, slo, hb, px, own, xch,
    ard, aru, sdn, sup, total, bsend, home,
    wsem, as_, ar_, ps_, pr_, gds, gdr, gus, gur, xs_, xr_, rds, rdr, rus, rur, bs_, br_,
):
    me = lax.axis_index("seq")
    z = lax.axis_index("ew")
    k = lax.rem(me, 2)
    e_me = lax.div(me, 2)
    partner = me + 1 - 2 * k
    experts, cap = picks_ref.shape
    tok, feat = tok_ref.shape
    slots = send.shape[3]
    starts = [sum(rows[:r]) for r in range(2)]
    last = n_ew - 1
    span = [pl.ds(starts[r], rows[r]) for r in range(2)]
    cut = [-(-rows[r] // 32) * 16 for r in range(2)]
    part = [
        p for r in range(2)
        for p in (pl.ds(starts[r], cut[r]), pl.ds(starts[r] + cut[r], rows[r] - cut[r]))
    ]
    within = [
        p for r in range(2) for p in (pl.ds(0, cut[r]), pl.ds(cut[r], rows[r] - cut[r]))
    ]

    barrier = pltpu.get_barrier_semaphore()
    for i in range(1, n_seq):
        pl.semaphore_signal(
            barrier, inc=1, device_id=(lax.rem(me + i, n_seq), z), device_id_type=MESH
        )

    @pl.when(z > 0)
    def _():
        pl.semaphore_signal(barrier, inc=1, device_id=(me, z - 1), device_id_type=MESH)

    @pl.when(z < last)
    def _():
        pl.semaphore_signal(barrier, inc=1, device_id=(me, z + 1), device_id_type=MESH)

    w_copies = [
        pltpu.make_async_copy(wout_ref, wv.at[0], wsem.at[0]),
        pltpu.make_async_copy(win_ref, wv.at[1], wsem.at[1]),
    ]
    for c in w_copies:
        c.start()

    base = (me * tok).astype(F32)
    local = picks_ref[...].astype(F32) - base
    pad = -experts % 8
    if pad:
        local = jnp.concatenate([local, jnp.full((pad, cap), -1.0, F32)], axis=0)
    local_c = jnp.transpose(local)
    t_row = iota((cap, tok), 1)
    hits = jnp.concatenate(
        [
            jnp.sum(jnp.where(local_c[:, e : e + 1] == t_row, 1.0, 0.0), axis=0, keepdims=True)
            for e in range(experts)
        ]
        + ([jnp.zeros((-experts % 16, tok), F32)] if experts % 16 else []),
        axis=0,
    )
    tri = jnp.where(iota((tok, tok), 0) < iota((tok, tok), 1), 1.0, 0.0).astype(BF16)
    keys = jnp.where(hits > 0.0, dot(hits.astype(BF16), tri), -1.0)
    for r in range(2):
        want = 2.0 * iota((slots, tok), 0) + float(r)
        for e in range(experts):
            pk[r, e] = jnp.where(want == keys[e : e + 1], 1.0, 0.0).astype(BF16)

    inside = (z > 0) & (z < last)

    @pl.when(inside)
    def _():
        pl.semaphore_wait(barrier, n_seq + 1)

    @pl.when(jnp.logical_not(inside))
    def _():
        pl.semaphore_wait(barrier, n_seq)

    def remote(src, dst, s, r, dev):
        return pltpu.make_async_remote_copy(
            src_ref=src, dst_ref=dst, send_sem=s, recv_sem=r, device_id=dev, device_id_type=MESH
        )

    def dispatch(r, i):
        d = lax.rem(me + i, n_seq)
        return remote(
            send.at[r, lax.rem(d, 2), lax.div(d, 2)], recv.at[r, me],
            as_.at[r, i], ar_.at[r, i], (d, z),
        )

    for r in range(2):
        sel = pk[r].reshape(experts * slots, tok)
        send[r, 0] = dot(sel, tok_ref[...]).astype(BF16).reshape(experts, slots, feat)
        send[r, 1] = dot(sel, cot_ref[...]).astype(BF16).reshape(experts, slots, feat)
        for i in range(1, n_seq):
            dispatch(r, i).start()
        recv[r, me] = send[r, k, e_me]

    pick = picks_ref[pl.ds(e_me, 1), :].astype(F32)
    owner = jnp.floor((pick + 0.5) * (1.0 / tok))
    cols = columns(pick, owner)
    rank = jnp.sum(
        jnp.where((cols[:, 1:2] == owner) & (cols[:, 0:1] < pick), 1.0, 0.0),
        axis=0, keepdims=True,
    )
    half = jnp.floor(rank * 0.5)
    cols = columns(owner * float(slots) + half, rank - 2.0 * half, gates_ref[pl.ds(e_me, 1), :])
    slot_c, parity, gate = cols[:, 0:1], cols[:, 1:2], cols[:, 2:3]
    wide = n_seq * slots
    before = jnp.where(iota((wide, wide), 0) < iota((wide, wide), 1), 1.0, 0.0).astype(BF16)
    for r in range(2):
        here = jnp.where(parity == float(r), slot_c, -1.0)
        match = here == iota((cap, wide), 1)
        valid = jnp.sum(jnp.where(match, 1.0, 0.0), axis=0, keepdims=True)
        gate_pad = jnp.sum(jnp.where(match, gate, 0.0), axis=0, keepdims=True)
        place = dot(jnp.broadcast_to(valid, (16, wide)).astype(BF16), before)[0:1]
        place = jnp.where(valid > 0.0, place, -1.0)
        pick_out = iota((rows[r], wide), 0) == place
        uu[span[r], :] = jnp.where(pick_out, 1.0, 0.0).astype(BF16)
        gcol[span[r], :] = jnp.sum(jnp.where(pick_out, gate_pad, 0.0), axis=1, keepdims=True)

    def compact(r):
        for i in range(1, n_seq):
            dispatch(r, i).wait_recv()
        full[k, z, span[r], :] = dot(
            uu[span[r], :], recv[r].reshape(wide, feat)
        ).astype(BF16)

    def g_down(u, h):
        ref = full.at[k, z + h, part[u]]
        return remote(ref, ref, gds.at[u, h], gdr.at[u, h], (me, z - 1))

    def g_up(u, h):
        ref = full.at[k, z - h, part[u]]
        return remote(ref, ref, gus.at[u, h], gur.at[u, h], (me, z + 1))

    def g_down_in(u, h):
        ref = full.at[k, z + 1 + h, part[u]]
        return remote(ref, ref, gds.at[u, h], gdr.at[u, h], (me, z + 1))

    def g_up_in(u, h):
        ref = full.at[k, z - 1 - h, part[u]]
        return remote(ref, ref, gus.at[u, h], gur.at[u, h], (me, z - 1))

    def g_pair(u, s, i, arr):
        ref = full.at[arr, s, part[u]]
        return remote(ref, ref, ps_.at[u, i], pr_.at[u, i], (partner, z))

    def gather_start(r):
        for u in (2 * r, 2 * r + 1):
            @pl.when(z > 0)
            def _():
                g_down(u, 0).start()

            @pl.when(z < last)
            def _():
                g_up(u, 0).start()

            g_pair(u, z, 0, k).start()

    def gather_arrive(r, h):
        for u in (2 * r, 2 * r + 1):
            @pl.when(z + 1 + h <= last)
            def _():
                g_down_in(u, h).wait_recv()
                if h + 1 <= last - 1:
                    @pl.when(z > 0)
                    def _():
                        g_down(u, h + 1).start()

                g_pair(u, z + 1 + h, 1 + 2 * h, k).start()

            @pl.when(z - 1 - h >= 0)
            def _():
                g_up_in(u, h).wait_recv()
                if h + 1 <= last - 1:
                    @pl.when(z < last)
                    def _():
                        g_up(u, h + 1).start()

                g_pair(u, z - 1 - h, 2 + 2 * h, k).start()

    def pair_sent(u):
        g_pair(u, z, 0, k).wait_send()
        for h in range(last):
            @pl.when(z + 1 + h <= last)
            def _():
                g_pair(u, z + 1 + h, 1 + 2 * h, k).wait_send()

            @pl.when(z - 1 - h >= 0)
            def _():
                g_pair(u, z - 1 - h, 2 + 2 * h, k).wait_send()

    def x_pair(r, j):
        return remote(
            px.at[j, span[r]], xch.at[j, span[r]], xs_.at[r, j], xr_.at[r, j], (partner, z)
        )

    def absorb_shard(r, s, i):
        n = rows[r]
        for u in (2 * r, 2 * r + 1):
            g_pair(u, s, i, 1 - k).wait_recv()
        cols = pl.ds(pl.multiple_of(s * feat, feat), feat)
        h_new = dot(full[0, s, span[r], :], wv[1, :, cols], (1, 1))
        s_new = dot(full[1, s, span[r], :], wv[0, :, cols], (1, 1))
        if i == 0:
            hid[0:n, :] = h_new
            slo[0:n, :] = s_new
        else:
            hid[0:n, :] += h_new
            slo[0:n, :] += s_new

    def absorb(r, h):
        if h < 0:
            absorb_shard(r, z, 0)
            return

        @pl.when(z + 1 + h <= last)
        def _():
            absorb_shard(r, z + 1 + h, 1 + 2 * h)

        @pl.when(z - 1 - h >= 0)
        def _():
            absorb_shard(r, z - 1 - h, 2 + 2 * h)

    def activate(r):
        n = rows[r]
        x = hid[0:n, :]
        cdf = 0.5 * (1.0 + lax.erf(x * math.sqrt(0.5)))
        pdf = jnp.exp(-0.5 * x * x) * (1.0 / math.sqrt(2.0 * math.pi))
        hb[0, 0:n, :] = (x * cdf).astype(BF16)
        hb[1, 0:n, :] = (slo[0:n, :] * (cdf + x * pdf)).astype(BF16)

    low = 2 * z < n_ew

    def project(r, i):
        n = rows[r]
        above = last - z
        j_low = jnp.where(i < above, last - i, i - above)
        j_high = jnp.where(i < z, i, last - (i - z))
        j = jnp.where(low, j_low, j_high) if i < last else z
        cols = pl.ds(pl.multiple_of(j * feat, feat), feat)
        px[j, span[r], :] = dot(hb[1 - k, 0:n, :], wv[1 - k, :, cols]).astype(BF16)
        x_pair(r, j).start()
        own[j, span[r], :] = dot(hb[k, 0:n, :], wv[k, :, cols]).astype(BF16)

    def r_down(u, j, t):
        return remote(sdn.at[j, part[u]], ard.at[j, part[u]], rds.at[u, t], rdr.at[u, t], (me, z - 1))

    def r_up(u, j, t):
        return remote(sup.at[j, part[u]], aru.at[j, part[u]], rus.at[u, t], rur.at[u, t], (me, z + 1))

    def r_down_in(u, j, t):
        return remote(sdn.at[j, part[u]], ard.at[j, part[u]], rds.at[u, t], rdr.at[u, t], (me, z + 1))

    def r_up_in(u, j, t):
        return remote(sup.at[j, part[u]], aru.at[j, part[u]], rus.at[u, t], rur.at[u, t], (me, z - 1))

    def pair_sum(u, j):
        return own[j, part[u], :].astype(F32) + xch[j, part[u], :].astype(F32)

    def reduce_step(r, t):
        jd = t - (last - z)

        @pl.when((jd >= 0) & (jd < z))
        def _():
            x_pair(r, jd).wait_recv()
            for u in (2 * r, 2 * r + 1):
                @pl.when(z == last)
                def _():
                    sdn[jd, part[u], :] = pair_sum(u, jd).astype(BF16)

                if t >= 1:
                    @pl.when(z < last)
                    def _():
                        r_down_in(u, jd, t - 1).wait_recv()
                        sdn[jd, part[u], :] = (
                            pair_sum(u, jd) + ard[jd, part[u], :].astype(F32)
                        ).astype(BF16)

                r_down(u, jd, t).start()

        ju = last - (t - z)

        @pl.when((ju > z) & (ju <= last))
        def _():
            x_pair(r, ju).wait_recv()
            for u in (2 * r, 2 * r + 1):
                @pl.when(z == 0)
                def _():
                    sup[ju, part[u], :] = pair_sum(u, ju).astype(BF16)

                if t >= 1:
                    @pl.when(z > 0)
                    def _():
                        r_up_in(u, ju, t - 1).wait_recv()
                        sup[ju, part[u], :] = (
                            pair_sum(u, ju) + aru[ju, part[u], :].astype(F32)
                        ).astype(BF16)

                r_up(u, ju, t).start()

    def give_back(r, i):
        d = lax.rem(me + i, n_seq)
        return remote(
            bsend.at[r, d], home.at[k, r, e_me], bs_.at[r, i], br_.at[r, i], (d, z)
        )

    def give_back_in(r, i):
        s = lax.rem(me + n_seq - i, n_seq)
        return remote(
            bsend.at[r, me], home.at[lax.rem(s, 2), r, lax.div(s, 2)],
            bs_.at[r, i], br_.at[r, i], (s, z),
        )

    def finish(r):
        n = rows[r]
        x_pair(r, z).wait_recv()
        for u in (2 * r, 2 * r + 1):
            total[within[u], :] = pair_sum(u, z)

            @pl.when(z < last)
            def _():
                r_down_in(u, z, last - 1).wait_recv()
                total[within[u], :] += ard[z, part[u], :].astype(F32)

            @pl.when(z > 0)
            def _():
                r_up_in(u, z, last - 1).wait_recv()
                total[within[u], :] += aru[z, part[u], :].astype(F32)

        term = (gcol[span[r], :] * total[0:n, :]).astype(BF16)
        bsend[r] = dot(uu[span[r], :], term, (0, 0)).astype(BF16).reshape(n_seq, slots, feat)
        for i in range(1, n_seq):
            give_back(r, i).start()
        home[k, r, e_me] = bsend[r, me]

    compact(0)
    gather_start(0)
    compact(1)
    for c in w_copies:
        c.wait()
    for h in range(last):
        if h == last - 1:
            gather_start(1)
        gather_arrive(0, h)
        absorb(0, h - 1)
    absorb(0, last - 1)
    activate(0)
    for i in range(last):
        project(0, i)
        gather_arrive(1, i)
        reduce_step(0, i)
        absorb(1, i - 1)
    project(0, last)
    absorb(1, last - 1)
    activate(1)
    for i in range(last):
        project(1, i)
        reduce_step(1, i)
        if i == 0:
            finish(0)
    project(1, last)
    finish(1)

    for r in range(2):
        for i in range(1, n_seq):
            give_back_in(r, i).wait_recv()
    sel = pk[...].reshape(2 * experts * slots, tok)
    out_ref[...] = dot(sel, home[0].reshape(2 * experts * slots, feat), (0, 0)).astype(BF16)
    grad_ref[...] = dot(sel, home[1].reshape(2 * experts * slots, feat), (0, 0)).astype(BF16)

    for r in range(2):
        for i in range(1, n_seq):
            dispatch(r, i).wait_send()
            give_back(r, i).wait_send()
        for j in range(n_ew):
            x_pair(r, j).wait_send()
    for u in range(4):
        pair_sent(u)
        for h in range(last):
            @pl.when((z > 0) & (z + h <= last))
            def _():
                g_down(u, h).wait_send()

            @pl.when((z < last) & (z - h >= 0))
            def _():
                g_up(u, h).wait_send()

            jd = h - (last - z)

            @pl.when((jd >= 0) & (jd < z))
            def _():
                r_down(u, jd, h).wait_send()

            ju = last - (h - z)

            @pl.when((ju > z) & (ju <= last))
            def _():
                r_up(u, ju, h).wait_send()


def per_device(tokens, cotangent, w_in, w_out, bar_picks, gate_weights):
    n_seq = lax.axis_size("seq")
    n_ew = lax.axis_size("ew")
    tok, feat = tokens.shape
    ff, depth = w_in.shape
    experts, cap = bar_picks.shape
    most = max(2, 2 * tok // n_seq)
    slots = -(-((most + 1) // 2) // 16) * 16
    rows = (-(-((cap + n_seq) // 2) // 16) * 16, -(-(cap // 2) // 16) * 16)
    both, top = sum(rows), max(rows)
    dma = pltpu.SemaphoreType.DMA
    vmem = pl.BlockSpec(memory_space=pltpu.VMEM)
    hbm = pl.BlockSpec(memory_space=pl.ANY)
    shape = jax.ShapeDtypeStruct((tok, feat), BF16)
    shards = pltpu.VMEM((n_ew, both, feat), BF16)
    steps = max(1, n_ew - 1)
    return tuple(
        pl.pallas_call(
            functools.partial(kernel, rows, n_seq, n_ew),
            out_shape=(shape, shape),
            in_specs=[vmem, vmem, hbm, hbm, vmem, vmem],
            out_specs=(vmem, vmem),
            scratch_shapes=[
                pltpu.VMEM((2, ff, depth), BF16),
                pltpu.VMEM((2, experts, slots, tok), BF16),
                pltpu.VMEM((both, n_seq * slots), BF16),
                pltpu.VMEM((both, 1), F32),
                pltpu.VMEM((2, 2, experts, slots, feat), BF16),
                pltpu.VMEM((2, n_seq, slots, feat), BF16),
                pltpu.VMEM((2, n_ew, both, feat), BF16),
                pltpu.VMEM((top, ff), F32),
                pltpu.VMEM((top, ff), F32),
                pltpu.VMEM((2, top, ff), BF16),
                shards, shards, shards,
                shards, shards, shards, shards,
                pltpu.VMEM((top, feat), F32),
                pltpu.VMEM((2, n_seq, slots, feat), BF16),
                pltpu.VMEM((2, 2, experts, slots, feat), BF16),
                dma((2,)),
                dma((2, n_seq)), dma((2, n_seq)),
                dma((4, 2 * steps + 1)), dma((4, 2 * steps + 1)),
                dma((4, steps)), dma((4, steps)), dma((4, steps)), dma((4, steps)),
                dma((2, n_ew)), dma((2, n_ew)),
                dma((4, steps)), dma((4, steps)), dma((4, steps)), dma((4, steps)),
                dma((2, n_seq)), dma((2, n_seq)),
            ],
            compiler_params=pltpu.CompilerParams(
                collective_id=0, has_side_effects=True, vmem_limit_bytes=56 * 1024 * 1024
            ),
        )(tokens, cotangent, w_in, w_out, bar_picks, gate_weights)
    )


def solution(mesh):
    in_specs = (
        P("seq", "ew"),
        P("seq", "ew"),
        P(("seq", "ew"), None),
        P(("seq", "ew"), None),
        P(),
        P(),
    )
    out_specs = (P("seq", "ew"), P("seq", "ew"))
    return jax.shard_map(
        per_device, mesh=mesh, in_specs=in_specs, out_specs=out_specs, check_vma=False
    )
```

time: 104 us -> 93.9 us (0.903)
  the two profiles are of different devices: /device:TPU:0 before, /device:TPU:25 now
where the time goes in v2:
time: 93.9 us; the launch traced here: 93.7 us
  Pallas kernels  89.3 us (95%)
  local copies, waits for them, and re-layouts  3.74 us (4%)
    pallas_call x1, Pallas kernels, per_device(): pl.pallas_call(functools.partial(kernel, rows, n_seq, n_ew), out_shape=(s...  89.3 us
    unnamed x2, local copies, waits for them, and re-layouts  3.74 us

profile of v2, /device:TPU:25, one launch (start us, length us, event | category | flops | bytes accessed | tf_op | source)
XLA Modules:
  0.0 93.7 jit_solution(1271168900396633601)
XLA Ops:
  0.6 89.3 %shard_map.77 = (bf16[256,1024]{1,0:T(8,128)(2,1)}, bf16[256,1024]{1,0:T(8,128)(2,1)}) custom-call(bf16[256,1024]{1,0:T(8,128)(2,1)} %tok_ref.1, bf16[256,1024]{1,0:T(8,128)(2,1)} %cot_ref.1, bf16[512,4096]{1,0:T(8,128)(2,1)} %win_ref.1, bf16[512,4096]{1,0:T(8,128)(2,1)} %wout_ref.1, s32[4,256]{1,0:T(4,128)} %picks_ref.1, f32[4,256]{1,0:T(4,128)} %gates_ref.1), custom_call_target="tpu_custom_call" | custom-call | tf_op jit(solution)/shard_map/pallas_call | solution.py:453
  90.0 1.9 %copy.10 = bf16[256,1024]{1,0:T(8,128)(2,1)} copy(bf16[256,1024]{1,0:T(8,128)(2,1)} %get-tuple-element.4) | data formatting | bytes 1048576
  91.8 1.9 %copy.11 = bf16[256,1024]{1,0:T(8,128)(2,1)} copy(bf16[256,1024]{1,0:T(8,128)(2,1)} %get-tuple-element.5) | data formatting | bytes 1048576
